TPU v7x, 128 devices: a whole 4x4x4 slice. The times are simulated.
128 devices in a mesh: face: 2 (over y_hi), tile: 64 (over x, z, y_lo, core).
Axes of the slice: x: 4, y: 4 (y_hi: 2, y_lo: 2; y = y_hi * 2 + y_lo), z: 4, core: 2. Of those that a mesh axis runs over, the one named last changes fastest.
Arguments:
- tracers: float32 [4, 32, 32, 8192], P(None, None, 'face', 'tile'), may hold values from -6 to 6
- wind_field: float32 [2, 32, 32, 8192], P(None, None, 'face', 'tile'), may hold values from -4 to 4
- metric: float32 [32, 8192], P('face', 'tile'), may hold values from 0.5 to 2
- forcing: bfloat16 [12, 44, 32, 8192], P(None, None, 'face', 'tile'), may hold values from -6 to 6
- aux_inputs: bfloat16 [384, 262144], P(None, ('face', 'tile')), may hold values from -6 to 6
- batch_pos: int32 [32, 8192], P('face', 'tile'), may hold values from 0 to 262143, as said below
- day_of_year: int32 [1], replicated, may hold values from 0 to 364
- w_in: bfloat16 [512, 556], replicated, may hold values from -0.25 to 0.25
- b_in: float32 [512], replicated, may hold values from -3 to 3
- w_mid: bfloat16 [512, 512], replicated, may hold values from -0.25 to 0.25
- b_mid: float32 [512], replicated, may hold values from -3 to 3
- w_out: bfloat16 [368, 512], replicated, may hold values from -0.25 to 0.25
- b_out: float32 [368], replicated, may hold values from -3 to 3
Outputs:
- updated: float32 [4, 32, 32, 8192], P(None, None, 'face', 'tile')
- diagnostics: bfloat16 [240, 262144], P(None, ('face', 'tile'))
Inputs may be any that keep to these rules, and one draw needn't show every extreme that they name: batch_pos is a permutation of all column positions. Number the devices d = (face index) * 64 + (tile index), device d holding batch positions d * 2048 to (d + 1) * 2048 - 1 and a block of 2048 grid columns. Of the grid columns of device s, exactly 16 have batch positions in the block of each device d, namely d * 2048 + s * 16 + j for j from 0 to 15.
All inputs are finite; a program needn't handle non-finite values.
Results may differ from a plain program's by a relative error of at most 0.012.
Values may be sent and summed in bfloat16 or wider, within the bound.
A program may use at most 128 MiB of HBM per device.

v0:
```python
import functools

import jax
import jax.numpy as jnp
import numpy as np
from jax import lax
from jax.experimental import pallas as pl
from jax.experimental.pallas import tpu as pltpu
from jax.sharding import PartitionSpec as P

SUBSTEPS = 4
FIELDS = 4
LEVELS = 32
HALF = 16
SIZE_X = 16
SIZE_Y = 128
COLUMNS = SIZE_X * SIZE_Y
CHANNELS = FIELDS * LEVELS
FORC = 44
AUX = 384
HIDDEN = 512
OUT = 368
HALO = 16
WIDE = SIZE_Y + 2 * HALO
NODES = WIDE // 4
CHUNK = 256
TILE_GROUPS = 4

MESH = pl.DeviceIdType.MESH
leak_slope = 0.15
time_step = 0.05
physics_weight = 0.5

root = np.sqrt(5.0)
big = 5.0 * (root + 1.0) / 4.0
mid = 5.0 * (root - 1.0) / 4.0
near = (root + 1.0) / 4.0
far = (root - 1.0) / 4.0


def derivative(s):
    c, d = s[0] - s[3], s[1] - s[2]
    e = (s[1] + s[2]) - (s[0] + s[3])
    p = (-1.75) * c + ((big + mid) / 2.0) * d
    q = (-(near - far) / 2.0) * c - (root / 4.0) * d
    outer, inner = 1.25 * e, (root / 4.0) * e
    return [p + outer, q + inner, q - inner, p - outer]


def leaky(value):
    return jnp.where(value > 0, value, leak_slope * value)


def iota(shape, dim):
    return lax.broadcasted_iota(jnp.int32, shape, dim)


def dot(a, b, contract=((1,), (0,))):
    return lax.dot_general(a, b, (contract, ((), ())), preferred_element_type=jnp.float32)


NT = ((1,), (1,))
TN = ((0,), (0,))


def kernel(
    tiles,
    tracers,
    winds,
    metric,
    forcing,
    aux,
    batch_pos,
    day,
    w_in,
    b_in,
    w_mid,
    b_mid,
    w_out,
    b_out,
    updated,
    diagnostics,
    tracers_v,
    winds_v,
    metric_v,
    forcing_v,
    aux_v,
    w_in_v,
    w_mid_v,
    w_out_v,
    load_sem,
    half_f32,
    half_b16,
    wind_b16,
    state_in,
    wind_in,
    halo_state,
    halo_wind,
    metric_all,
    pos_all,
    state,
    wind,
    mass,
    inverse,
    rate,
    place,
    forc_rows,
    forc_mat,
    forc_out,
    forc_in,
    dyn,
    dyn_out,
    dyn_in,
    back_out,
    back_in,
    pre,
    w_aux,
    w_dyn,
    bias_in,
    bias_mid,
    bias_out,
    diag_v,
    total,
    updated_v,
    near_send,
    near_recv,
    halo_send,
    halo_recv,
    relay_send,
    forc_recv,
    dyn_recv,
    back_recv,
    out_sem,
):
    devices = 2 * tiles
    per_peer = COLUMNS // devices
    group = tiles // TILE_GROUPS
    f = lax.axis_index("face")
    t = lax.axis_index("tile")
    me = f * tiles + t
    u_me = t // group
    k_me = t % group
    right = lax.rem(t + 1, tiles)
    left = lax.rem(t + tiles - 1, tiles)
    other = 1 - f

    def at(p):
        return (p // tiles, lax.rem(p, tiles))

    def own_rows(p):
        return pl.ds(pl.multiple_of(p * per_peer, 16), per_peer)

    loads = [
        pltpu.make_async_copy(a, b, load_sem.at[i])
        for i, (a, b) in enumerate(
            (
                (winds, winds_v),
                (tracers, tracers_v),
                (metric, metric_v),
                (w_in, w_in_v),
                (aux, aux_v),
                (forcing, forcing_v),
                (w_mid, w_mid_v),
                (w_out, w_out_v),
            )
        )
    ]
    for load in loads:
        load.start()

    barrier = pltpu.get_barrier_semaphore()

    @pl.loop(1, devices)
    def _(k):
        p = lax.rem(me + k, devices)
        pl.semaphore_signal(barrier, inc=1, device_id=at(p), device_id_type=MESH)

    loads[0].wait()
    for h in range(2):
        for g in range(4):
            rows = [
                winds_v[pl.ds(c * 512 + h * 256 + xh * 8 + 2 * g + lo, HALF, stride=SIZE_X), :]
                for c in range(2)
                for lo in range(2)
                for xh in range(2)
            ]
            wind_b16[h, g] = jnp.concatenate(rows, axis=0).T.astype(jnp.bfloat16)
    loads[1].wait()
    for h in range(2):
        for x in range(8):
            rows = [
                tracers_v[pl.ds(i * 512 + h * 256 + xh * 8 + x, HALF, stride=SIZE_X), :]
                for xh in range(2)
                for i in range(FIELDS)
            ]
            turned = jnp.concatenate(rows, axis=0).T
            half_f32[h, x] = turned
            half_b16[h, x] = turned.astype(jnp.bfloat16)
    loads[2].wait()
    face_rows = pl.ds(pl.multiple_of(f * SIZE_X, SIZE_X), SIZE_X)
    metric_all[0, face_rows, :] = metric_v[...]
    pos_all[f] = batch_pos[...]

    pl.semaphore_wait(barrier, devices - 1)

    def remote(src, dst, send, recv, target):
        copy = pltpu.make_async_remote_copy(
            src, dst, send, recv, device_id=target, device_id_type=MESH
        )
        copy.start()
        return copy

    def arrived(ref, sem):
        pltpu.make_async_copy(ref, ref, sem).wait()

    partner = (other, t)
    sent = [
        remote(metric_v, metric_all.at[0, face_rows], near_send.at[0], near_recv.at[0], partner),
        remote(batch_pos, pos_all.at[f], near_send.at[1], near_recv.at[1], partner),
    ]
    sides = ((0, right, SIZE_Y - HALO), (1, left, 0))
    for face in range(2):
        for side, tile, start in sides:
            rows = pl.ds(start, HALO)
            for kind, src, dst in (
                (0, metric_v, metric_all.at[1 + side, face_rows]),
                (1, wind_b16.at[face, :, rows], halo_wind.at[side, f]),
                (2, half_b16.at[face, :, rows], halo_state.at[side, f]),
            ):
                sent.append(
                    remote(
                        src,
                        dst,
                        halo_send.at[kind, side, face],
                        halo_recv.at[kind, side, f],
                        (face, tile),
                    )
                )
    sent.append(remote(wind_b16.at[other], wind_in.at[f], near_send.at[2], near_recv.at[2], partner))
    sent.append(remote(half_b16.at[other], state_in.at[f], near_send.at[3], near_recv.at[3], partner))

    def fill_place(face):
        pos = pos_all[face]
        slot = pos // COLUMNS * per_peer + pos % per_peer

        @pl.loop(0, COLUMNS // CHUNK)
        def _(i):
            rows = pl.ds(pl.multiple_of(i * CHUNK, CHUNK), CHUNK)
            index = iota((CHUNK, SIZE_Y), 0)
            here = slot - i * CHUNK
            for x in range(SIZE_X):
                hit = index == here[x : x + 1, :]
                place[face, rows, x * SIZE_Y : (x + 1) * SIZE_Y] = hit.astype(jnp.bfloat16)

    fill_place(f)

    loads[5].wait()
    months = day[0] * 12
    month_lo = months // 365
    month_hi = lax.rem(month_lo + 1, 12)
    part = jnp.full((1, 1, SIZE_Y), months - month_lo * 365, jnp.int32).astype(jnp.float32) / 365.0
    for c in range(0, FORC, 4):
        lower = forcing_v[pl.ds(month_lo * FORC + c, 4)].astype(jnp.float32)
        upper = forcing_v[pl.ds(month_hi * FORC + c, 4)].astype(jnp.float32)
        now = (1.0 - part) * lower + part * upper
        forc_rows[c * SIZE_X : (c + 4) * SIZE_X, :] = now.reshape(4 * SIZE_X, SIZE_Y)
    forc_rows[FORC * SIZE_X :, :] = jnp.zeros((4 * SIZE_X, SIZE_Y), jnp.float32)
    forc_mat[48:, :] = jnp.zeros((80, COLUMNS), jnp.bfloat16)
    for x in range(SIZE_X):
        forc_mat[0:48, x * SIZE_Y : (x + 1) * SIZE_Y] = forc_rows[
            pl.ds(x, 48, stride=SIZE_X), :
        ].astype(jnp.bfloat16)

    def spread(first, out, dst, recv):
        @pl.loop(0, group)
        def _(k):
            p = first + lax.rem(k_me + k, group)

            @pl.when(p != me)
            def _():
                pltpu.make_async_remote_copy(
                    out.at[own_rows(p)],
                    dst.at[own_rows(me)],
                    relay_send,
                    recv,
                    device_id=at(p),
                    device_id_type=MESH,
                ).start()

            @pl.when(p == me)
            def _():
                pltpu.make_async_copy(out.at[own_rows(me)], dst.at[own_rows(me)], recv).start()

    @pl.loop(0, COLUMNS // CHUNK)
    def _(i):
        c = lax.rem(u_me + i, 2 * TILE_GROUPS)
        rows = pl.ds(pl.multiple_of(c * CHUNK, CHUNK), CHUNK)
        forc_out[rows, :] = dot(place[f, rows, :], forc_mat[...], NT).astype(jnp.bfloat16)
        spread(c * group, forc_out, forc_in, forc_recv)

    def spread_bias(ref, into, size):
        for k in range(0, size, 128):
            n = min(128, size - k)
            into[k : k + n, :] = jnp.broadcast_to(ref[:, k : k + n], (128, n)).T

    spread_bias(b_in, bias_in, HIDDEN)
    spread_bias(b_mid, bias_mid, HIDDEN)
    spread_bias(b_out, bias_out, OUT)
    loads[3].wait()
    w_aux[...] = w_in_v[:, CHANNELS + FORC :]
    lane = iota((CHANNELS, 512), 1)
    ch = (lane // 16) % 4 * LEVELS + lane // 128 % 2 * HALF + lane % 16
    pick = (iota((CHANNELS, 512), 0) == ch) & (lane // 64 % 2 == lane // 256)
    w_dyn[...] = dot(w_in_v[:, 0:CHANNELS], pick.astype(jnp.bfloat16)).astype(jnp.bfloat16)
    loads[4].wait()

    def twice(value):
        return jnp.concatenate([value, value], axis=1)

    @pl.loop(0, COLUMNS // CHUNK)
    def _(i):
        cols = pl.ds(pl.multiple_of(i * CHUNK, CHUNK), CHUNK)
        pre[:, cols] = dot(w_aux[...], aux_v[:, cols]) + twice(bias_in[...])

    arrived(metric_all.at[0, pl.ds(0, SIZE_X)], near_recv.at[0])
    for face in range(2):
        for side in range(2):
            arrived(metric_all.at[1 + side, pl.ds(0, SIZE_X)], halo_recv.at[0, side, face])

    def node_weight(shape, dim):
        n = iota(shape, dim) % 4
        return jnp.where((n == 0) | (n == 3), np.float32(1.0 / 6.0), np.float32(5.0 / 6.0))

    turned = []
    for k in range(3):
        block = metric_all[k] * node_weight((32, SIZE_Y), 0) * node_weight((32, SIZE_Y), 1)
        turned.append(jnp.concatenate([block] * 4, axis=0).T)
    points = jnp.concatenate([turned[0], turned[2][:HALO], turned[1][SIZE_Y - HALO :]], axis=0)
    node_x = iota((WIDE, 128), 1) % 4
    node_y = iota((WIDE, 128), 0) % 4
    along = points + jnp.where(node_x == 0, pltpu.roll(points, 1, 1), 0.0)
    along = along + jnp.where(node_x == 3, pltpu.roll(points, 127, 1), 0.0)
    both = along + jnp.where(node_y == 0, pltpu.roll(along, 1, 0), 0.0)
    both = both + jnp.where(node_y == 3, pltpu.roll(along, WIDE - 1, 0), 0.0)
    scaled, inverted = -time_step * points, 1.0 / both
    low = iota((WIDE, 128), 1) < 64
    for face in range(2):
        for x in range(8):
            k = face * SIZE_X + x
            for value, into in ((scaled, mass), (inverted, inverse)):
                one = jnp.broadcast_to(value[:, k : k + 1], (WIDE, 128))
                two = jnp.broadcast_to(value[:, k + 8 : k + 9], (WIDE, 128))
                into[face, x] = jnp.where(low, one, two)

    arrived(pos_all.at[0], near_recv.at[1])
    fill_place(other)

    wind_in[f] = wind_b16[f]
    state[f, :, 0:SIZE_Y, :] = half_f32[f]
    out_lane = iota((128, 512), 1)
    from_lane = out_lane // 128 * 32 + out_lane // 64 % 2 * 16 + out_lane % 16
    widen = (iota((128, 512), 0) == from_lane).astype(jnp.bfloat16)
    for kind in (1, 2):
        for face in range(2):
            for side in range(2):
                ref = (halo_wind, halo_state)[kind - 1].at[side, face]
                arrived(ref, halo_recv.at[kind, side, face])
    arrived(wind_in.at[0], near_recv.at[2])
    for face in range(2):
        for g in range(4):
            rows = jnp.concatenate(
                [wind_in[face, g], halo_wind[1, face, g], halo_wind[0, face, g]], axis=0
            )
            wide = dot(rows, widen)
            for c in range(2):
                for lo in range(2):
                    k = 2 * c + lo
                    x = 2 * g + lo
                    wind[c, face, x] = wide[:, k * 128 : (k + 1) * 128] * mass[face, x]
    for face in range(2):
        state[face, :, SIZE_Y : SIZE_Y + HALO, :] = halo_state[1, face].astype(jnp.float32)
        state[face, :, SIZE_Y + HALO :, :] = halo_state[0, face].astype(jnp.float32)
    arrived(state_in.at[0], near_recv.at[3])
    state[other, :, 0:SIZE_Y, :] = state_in[other].astype(jnp.float32)

    low_half = iota((NODES, 128), 1) < 64

    @pl.loop(0, SUBSTEPS)
    def _(step):
        @pl.loop(0, NODES // 8)
        def _(i):
            for face in range(2):
                for e in range(0, 8, 4):

                    def rows(j):
                        return pl.ds(i * 32 + j, 8, stride=4)

                    s = [[state[face, e + a, rows(j), :] for j in range(4)] for a in range(4)]
                    along_y = [derivative(s[a]) for a in range(4)]
                    for j in range(4):
                        along_x = derivative([s[a][j] for a in range(4)])
                        for a in range(4):
                            value = wind[0, face, e + a, rows(j), :] * along_x[a]
                            value = value + wind[1, face, e + a, rows(j), :] * along_y[a][j]
                            rate[face, e + a, j, pl.ds(pl.multiple_of(i * 8, 8), 8), :] = value

        def summed(face, x, j):
            value = rate[face, x, j]
            if x == 3:
                return value + rate[face, 4, j]
            if x == 4:
                return rate[face, 3, j] + value
            if x == 7:
                pair = jnp.where(low_half, rate[1 - face, 0, j], rate[face, 0, j])
                return value + pltpu.roll(pair, 64, 1)
            if x == 0:
                pair = jnp.where(low_half, rate[face, 7, j], rate[1 - face, 7, j])
                return value + pltpu.roll(pair, 64, 1)
            return value

        for face in range(2):
            for x in range(8):
                z = [summed(face, x, j) for j in range(4)]
                z[0], z[3] = (
                    z[0] + pltpu.roll(z[3], 1, 0),
                    z[3] + pltpu.roll(z[0], NODES - 1, 0),
                )
                for j in range(4):
                    rows = pl.ds(j, NODES, stride=4)
                    state[face, x, rows, :] = (
                        state[face, x, rows, :] + z[j] * inverse[face, x, rows, :]
                    )

    for face in range(2):
        for x in range(8):
            dyn[face, x * SIZE_Y : (x + 1) * SIZE_Y, :] = state[face, x, 0:SIZE_Y, :].astype(
                jnp.bfloat16
            )

    low_row = iota((CHUNK, 128), 1) < 64

    @pl.loop(0, 2 * TILE_GROUPS)
    def _(i):
        c = lax.rem(i, 2) * TILE_GROUPS + lax.rem(u_me + TILE_GROUPS - i // 2, TILE_GROUPS)
        rows = pl.ds(pl.multiple_of(c * CHUNK, CHUNK), CHUNK)
        q = [
            [dot(place[face, rows, xh * 1024 : (xh + 1) * 1024], dyn[face]) for xh in range(2)]
            for face in range(2)
        ]
        turn = pltpu.roll(jnp.where(low_row, q[1][0], q[0][1]), 64, 1)
        dyn_out[rows, :] = (jnp.where(low_row, q[0][0], q[1][1]) + turn).astype(jnp.bfloat16)
        spread(c * group, dyn_out, dyn_in, dyn_recv.at[f * TILE_GROUPS + u_me])

    arrived(forc_in, forc_recv)

    @pl.loop(0, COLUMNS // CHUNK)
    def _(i):
        cols = pl.ds(pl.multiple_of(i * CHUNK, CHUNK), CHUNK)
        pre[:, cols] += dot(w_in_v[:, CHANNELS : 2 * CHANNELS], forc_in[cols, :], NT)

    loads[6].wait()
    loads[7].wait()
    level_lane = iota((256, CHANNELS), 1)
    level_row = iota((256, CHANNELS), 0)

    @pl.loop(0, TILE_GROUPS)
    def _(v):
        u = lax.rem(u_me + v, TILE_GROUPS)
        halves = []
        for h in range(2):
            c = h * TILE_GROUPS + u
            rows = pl.ds(pl.multiple_of(c * CHUNK, CHUNK), CHUNK)
            arrived(dyn_in.at[rows], dyn_recv.at[c])
            halves.append(dyn_in[rows, :])
        block = jnp.concatenate(halves, axis=1)
        for face in range(2):
            c = face * TILE_GROUPS + u
            cols = pl.ds(pl.multiple_of(c * CHUNK, CHUNK), CHUNK)
            hidden = pre[:, cols] + dot(w_dyn[:, face * 256 : (face + 1) * 256], block, NT)
            hidden = leaky(hidden).astype(jnp.bfloat16)
            hidden = dot(w_mid_v[...], hidden) + twice(bias_mid[...])
            hidden = leaky(hidden).astype(jnp.bfloat16)
            result = dot(w_out_v[...], hidden) + twice(bias_out[...])
            result = result.astype(jnp.bfloat16)
            diag_v[:, cols] = result[CHANNELS:, :]
            row = level_lane // LEVELS * 16 + level_lane % 16
            row = row + level_lane // HALF % 2 * 128 + face * 64
            pick = (level_row == row).astype(jnp.bfloat16)
            change = result[0:CHANNELS, :].astype(jnp.float32).T
            value = dot(block, pick) + physics_weight * change
            back_out[cols, :] = value.astype(jnp.bfloat16)
            spread(c * group, back_out, back_in, back_recv.at[f * TILE_GROUPS + u_me])

    diag_copy = pltpu.make_async_copy(diag_v, diagnostics, out_sem.at[0])
    diag_copy.start()

    for v in range(TILE_GROUPS):
        u = lax.rem(u_me + TILE_GROUPS - v, TILE_GROUPS)
        for face in range(2):
            c = face * TILE_GROUPS + u
            rows = pl.ds(pl.multiple_of(c * CHUNK, CHUNK), CHUNK)
            arrived(back_in.at[rows], back_recv.at[c])
            back = back_in[rows, :]
            for k in range(0, COLUMNS, 512):
                value = dot(back, place[f, rows, k : k + 512], TN)
                if v == 0 and face == 0:
                    total[:, k : k + 512] = value
                elif v < TILE_GROUPS - 1 or face == 0:
                    total[:, k : k + 512] += value
                else:
                    value = total[:, k : k + 512] + value
                    for x in range(4):
                        updated_v[pl.ds(k // SIZE_Y + x, CHANNELS, stride=SIZE_X), :] = value[
                            :, x * SIZE_Y : (x + 1) * SIZE_Y
                        ]
    updated_copy = pltpu.make_async_copy(updated_v, updated, out_sem.at[1])
    updated_copy.start()
    for copy in sent:
        copy.wait_send()
    away = pl.ds(0, (devices - 1) * per_peer)
    for out in (forc_out, dyn_out, back_out):
        arrived(out.at[away], relay_send)
    diag_copy.wait()
    updated_copy.wait()


def local(
    tracers,
    wind_field,
    metric,
    forcing,
    aux_inputs,
    batch_pos,
    day_of_year,
    w_in,
    b_in,
    w_mid,
    b_mid,
    w_out,
    b_out,
):
    tiles = lax.axis_size("tile")
    anywhere = pl.BlockSpec(memory_space=pl.ANY)
    vmem = pl.BlockSpec(memory_space=pltpu.VMEM)
    f32, b16 = jnp.float32, jnp.bfloat16
    dma = pltpu.SemaphoreType.DMA
    scratch = [
        pltpu.VMEM((CHANNELS * SIZE_X, SIZE_Y), f32),
        pltpu.VMEM((2 * LEVELS * SIZE_X, SIZE_Y), f32),
        pltpu.VMEM((SIZE_X, SIZE_Y), f32),
        pltpu.VMEM((12 * FORC, SIZE_X, SIZE_Y), b16),
        pltpu.VMEM((AUX, COLUMNS), b16),
        pltpu.VMEM(w_in.shape, b16),
        pltpu.VMEM(w_mid.shape, b16),
        pltpu.VMEM(w_out.shape, b16),
        dma((8,)),
        pltpu.VMEM((2, 8, SIZE_Y, 128), f32),
        pltpu.VMEM((2, 8, SIZE_Y, 128), b16),
        pltpu.VMEM((2, 4, SIZE_Y, 128), b16),
        pltpu.VMEM((2, 8, SIZE_Y, 128), b16),
        pltpu.VMEM((2, 4, SIZE_Y, 128), b16),
        pltpu.VMEM((2, 2, 8, HALO, 128), b16),
        pltpu.VMEM((2, 2, 4, HALO, 128), b16),
        pltpu.VMEM((3, 2 * SIZE_X, SIZE_Y), f32),
        pltpu.VMEM((2, SIZE_X, SIZE_Y), jnp.int32),
        pltpu.VMEM((2, 8, WIDE, 128), f32),
        pltpu.VMEM((2, 2, 8, WIDE, 128), f32),
        pltpu.VMEM((2, 8, WIDE, 128), f32),
        pltpu.VMEM((2, 8, WIDE, 128), f32),
        pltpu.VMEM((2, 8, 4, NODES, 128), f32),
        pltpu.VMEM((2, COLUMNS, COLUMNS), b16),
        pltpu.VMEM((48 * SIZE_X, SIZE_Y), f32),
        pltpu.VMEM((128, COLUMNS), b16),
        pltpu.VMEM((COLUMNS, 128), b16),
        pltpu.VMEM((COLUMNS, 128), b16),
        pltpu.VMEM((2, COLUMNS // 2, 128), b16),
        pltpu.VMEM((COLUMNS, 128), b16),
        pltpu.VMEM((COLUMNS, 128), b16),
        pltpu.VMEM((COLUMNS, 128), b16),
        pltpu.VMEM((COLUMNS, 128), b16),
        pltpu.VMEM((HIDDEN, COLUMNS), f32),
        pltpu.VMEM((HIDDEN, AUX), b16),
        pltpu.VMEM((HIDDEN, 512), b16),
        pltpu.VMEM((HIDDEN, 128), f32),
        pltpu.VMEM((HIDDEN, 128), f32),
        pltpu.VMEM((OUT, 128), f32),
        pltpu.VMEM((OUT - CHANNELS, COLUMNS), b16),
        pltpu.VMEM((CHANNELS, COLUMNS), f32),
        pltpu.VMEM((CHANNELS * SIZE_X, SIZE_Y), f32),
        dma((4,)),
        dma((4,)),
        dma((3, 2, 2)),
        dma((3, 2, 2)),
        dma,
        dma,
        dma((2 * TILE_GROUPS,)),
        dma((2 * TILE_GROUPS,)),
        dma((2,)),
    ]
    updated, diagnostics = pl.pallas_call(
        functools.partial(kernel, tiles),
        out_shape=(
            jax.ShapeDtypeStruct((CHANNELS * SIZE_X, SIZE_Y), f32),
            jax.ShapeDtypeStruct((OUT - CHANNELS, COLUMNS), b16),
        ),
        in_specs=[
            anywhere,
            anywhere,
            anywhere,
            anywhere,
            anywhere,
            vmem,
            pl.BlockSpec(memory_space=pltpu.SMEM),
            anywhere,
            vmem,
            anywhere,
            vmem,
            anywhere,
            vmem,
        ],
        out_specs=(anywhere, anywhere),
        scratch_shapes=scratch,
        compiler_params=pltpu.CompilerParams(
            collective_id=0, has_side_effects=True, vmem_limit_bytes=60 * 2**20
        ),
    )(
        tracers.reshape(CHANNELS * SIZE_X, SIZE_Y),
        wind_field.reshape(2 * LEVELS * SIZE_X, SIZE_Y),
        metric,
        forcing.reshape(12 * FORC, SIZE_X, SIZE_Y),
        aux_inputs,
        batch_pos,
        day_of_year,
        w_in,
        b_in.reshape(1, HIDDEN),
        w_mid,
        b_mid.reshape(1, HIDDEN),
        w_out,
        b_out.reshape(1, OUT),
    )
    return updated.reshape(tracers.shape), diagnostics


def solution(mesh):
    placed = (
        P(None, None, "face", "tile"),
        P(None, None, "face", "tile"),
        P("face", "tile"),
        P(None, None, "face", "tile"),
        P(None, ("face", "tile")),
        P("face", "tile"),
        P(),
        P(),
        P(),
        P(),
        P(),
        P(),
        P(),
    )
    return jax.shard_map(
        local,
        mesh=mesh,
        in_specs=placed,
        out_specs=(P(None, None, "face", "tile"), P(None, ("face", "tile"))),
        check_vma=False,
    )
```

profile of v0, /device:TPU:1, one launch (start us, length us, event | category | flops | bytes accessed | tf_op | source)
XLA Modules:
  0.0 70.4 jit_solution(8961850772003619936)
XLA Ops:
  1.3 1.2 %reshape.30.b_out = f32[1,368]{1,0:T(1,128)} reshape(f32[368]{0:T(512)} %param.25) | data formatting | bytes 2944 | tf_op jit(solution)/shard_map/reshape | solution.py:639
  2.5 2.1 %copy.15.w_in = bf16[512,556]{1,0:T(8,128)(2,1)} copy(bf16[512,556]{0,1:T(8,128)(2,1)} %param.20) | data formatting | bytes 1138688 | tf_op args[7]
  4.7 62.4 %shard_map.140 = (f32[2048,128]{1,0:T(8,128)}, bf16[240,2048]{1,0:T(8,128)(2,1)}) custom-call(f32[2048,128]{1,0:T(8,128)} %bitcast.8, f32[1024,128]{1,0:T(8,128)} %bitcast.9, f32[16,128]{1,0:T(8,128)} %metric.1, bf16[528,16,128]{2,1,0:T(8,128)(2,1)} %bitcast.6, bf16[384,2048]{1,0:T(8,128)(2,1)} %aux.1, s32[16,128]{1,0:T(8,128)} %batch_pos.1, ...), custom_call_target="tpu_custom_call" | custom-call | tf_op jit(solution)/shard_map/pallas_call | solution.py:600
  67.0 0.0 copy-start
  67.0 2.4 %copy.19 = f32[4,32,16,128]{3,2,1,0:T(8,128)} copy(f32[4,32,16,128]{3,2,1,0:T(8,128)} %bitcast.7) | data formatting | bytes 2097152
  69.4 0.0 copy-done
  69.4 0.9 %copy.20 = bf16[240,2048]{1,0:T(8,128)(2,1)} copy(bf16[240,2048]{1,0:T(8,128)(2,1)S(1)} %copy-done) | data formatting | bytes 1966080
Async XLA Ops:
  67.0 2.4 %copy-start = (bf16[240,2048]{1,0:T(8,128)(2,1)S(1)}, bf16[240,2048]{1,0:T(8,128)(2,1)}, u32[]{:S(2)}) copy-start(bf16[240,2048]{1,0:T(8,128)(2,1)} %get-tuple-element.9) | copy-start | bytes 2949124
where the time goes:
time: 70.7 us; the launch traced here: 70.4 us
  Pallas kernels  62.4 us (88%)
  local copies, waits for them, and re-layouts  6.7 us (9%)
  between operations  1.29 us (2%)
    pallas_call x1, Pallas kernels, local(): pl.pallas_call(functools.partial(kernel, tiles), out_shape=(jax.ShapeDtyp...  62.4 us
    unnamed x5, local copies, waits for them, and re-layouts  5.45 us

commit v1 on v0

--- a/solution.py
+++ b/solution.py
@@ -57,6 +57,12 @@
 
 def dot(a, b, contract=((1,), (0,))):
     return lax.dot_general(a, b, (contract, ((), ())), preferred_element_type=jnp.float32)
+
+
+def stage(i):
+    a = (i + 2) // 4
+    pair = a % 2
+    return 2 - a + pair * 2 * (i % 2), pair * ((i + 2) // 2 - 2) + (1 - pair) * (i % 2)
 
 
 NT = ((1,), (1,))
@@ -115,18 +121,19 @@
     back_in,
     pre,
     w_aux,
+    w_forc,
     w_dyn,
     bias_in,
     bias_mid,
     bias_out,
     diag_v,
     total,
-    updated_v,
     near_send,
     near_recv,
     halo_send,
     halo_recv,
     relay_send,
+    forc_send,
     forc_recv,
     dyn_recv,
     back_recv,
@@ -265,53 +272,87 @@
         now = (1.0 - part) * lower + part * upper
         forc_rows[c * SIZE_X : (c + 4) * SIZE_X, :] = now.reshape(4 * SIZE_X, SIZE_Y)
     forc_rows[FORC * SIZE_X :, :] = jnp.zeros((4 * SIZE_X, SIZE_Y), jnp.float32)
-    forc_mat[48:, :] = jnp.zeros((80, COLUMNS), jnp.bfloat16)
     for x in range(SIZE_X):
-        forc_mat[0:48, x * SIZE_Y : (x + 1) * SIZE_Y] = forc_rows[
-            pl.ds(x, 48, stride=SIZE_X), :
-        ].astype(jnp.bfloat16)
-
-    def spread(first, out, dst, recv):
-        @pl.loop(0, group)
-        def _(k):
-            p = first + lax.rem(k_me + k, group)
-
-            @pl.when(p != me)
-            def _():
-                pltpu.make_async_remote_copy(
-                    out.at[own_rows(p)],
-                    dst.at[own_rows(me)],
-                    relay_send,
-                    recv,
-                    device_id=at(p),
-                    device_id_type=MESH,
-                ).start()
-
-            @pl.when(p == me)
-            def _():
-                pltpu.make_async_copy(out.at[own_rows(me)], dst.at[own_rows(me)], recv).start()
+        block = forc_rows[pl.ds(x, 48, stride=SIZE_X), :].astype(jnp.bfloat16)
+        for k in (0, 64):
+            forc_mat[k : k + 48, x * SIZE_Y : (x + 1) * SIZE_Y] = block
+    for k in (48, 112):
+        forc_mat[k : k + 16, :] = jnp.zeros((16, COLUMNS), jnp.bfloat16)
+
+    def spread(c, out, dst, recv):
+        def send(k):
+            p = c * group + lax.rem(k_me + k, group)
+            pltpu.make_async_remote_copy(
+                out.at[own_rows(p)],
+                dst.at[own_rows(me)],
+                relay_send,
+                recv,
+                device_id=at(p),
+                device_id_type=MESH,
+            ).start()
+
+        own = c == f * TILE_GROUPS + u_me
+
+        @pl.when(own)
+        def _():
+            for k in range(1, group):
+                send(k)
+            pltpu.make_async_copy(out.at[own_rows(me)], dst.at[own_rows(me)], recv).start()
+
+        @pl.when(jnp.logical_not(own))
+        def _():
+            for k in range(group):
+                send(k)
+
+    chips = devices // 2
+    core = lax.rem(t, 2)
+    low_lane = iota((per_peer, 128), 1) < 64
+
+    def chip_rows(g):
+        return pl.ds(pl.multiple_of(g * per_peer, 16), per_peer)
 
     @pl.loop(0, COLUMNS // CHUNK)
     def _(i):
-        c = lax.rem(u_me + i, 2 * TILE_GROUPS)
-        rows = pl.ds(pl.multiple_of(c * CHUNK, CHUNK), CHUNK)
-        forc_out[rows, :] = dot(place[f, rows, :], forc_mat[...], NT).astype(jnp.bfloat16)
-        spread(c * group, forc_out, forc_in, forc_recv)
+        n = CHUNK // per_peer
+        rows = pl.ds(pl.multiple_of(i * CHUNK, CHUNK), CHUNK)
+        value = dot(place[f, rows, :], forc_mat[...], NT)
+        for k in range(0, max(n, 1), 2):
+            both = [value[(k + m) * per_peer : (k + m + 1) * per_peer, :] for m in range(2)]
+            packed = jnp.where(low_lane, both[0], both[1]).astype(jnp.bfloat16)
+            forc_out[chip_rows((i * n + k) // 2), :] = packed
+
+    chip = me // 2
+
+    def send_forcing(k):
+        g = lax.rem(chip + k, chips)
+        pltpu.make_async_remote_copy(
+            forc_out.at[chip_rows(g)],
+            forc_in.at[core, chip_rows(chip)],
+            forc_send.at[0],
+            forc_recv.at[0],
+            device_id=at(2 * g + core),
+            device_id_type=MESH,
+        ).start()
 
     def spread_bias(ref, into, size):
         for k in range(0, size, 128):
             n = min(128, size - k)
-            into[k : k + n, :] = jnp.broadcast_to(ref[:, k : k + n], (128, n)).T
+            into[k : k + n, :] = jnp.broadcast_to(ref[k : k + n].reshape(1, n), (128, n)).T
 
     spread_bias(b_in, bias_in, HIDDEN)
     spread_bias(b_mid, bias_mid, HIDDEN)
     spread_bias(b_out, bias_out, OUT)
     loads[3].wait()
-    w_aux[...] = w_in_v[:, CHANNELS + FORC :]
+    w_aux[...] = w_in_v[CHANNELS + FORC :, :].T
+    row = iota((CHANNELS, 128), 0)
+    pick = (iota((CHANNELS, 128), 1) == row + core * 64) & (row < FORC)
+    w_forc[...] = dot(
+        w_in_v[CHANNELS : 2 * CHANNELS, :], pick.astype(jnp.bfloat16), TN
+    ).astype(jnp.bfloat16)
     lane = iota((CHANNELS, 512), 1)
     ch = (lane // 16) % 4 * LEVELS + lane // 128 % 2 * HALF + lane % 16
     pick = (iota((CHANNELS, 512), 0) == ch) & (lane // 64 % 2 == lane // 256)
-    w_dyn[...] = dot(w_in_v[:, 0:CHANNELS], pick.astype(jnp.bfloat16)).astype(jnp.bfloat16)
+    w_dyn[...] = dot(w_in_v[0:CHANNELS, :], pick.astype(jnp.bfloat16), TN).astype(jnp.bfloat16)
     loads[4].wait()
 
     def twice(value):
@@ -387,6 +428,20 @@
 
     @pl.loop(0, SUBSTEPS)
     def _(step):
+        few = chips // SUBSTEPS
+        for k in range(1, few):
+            send_forcing(step * few + k)
+
+        @pl.when(step > 0)
+        def _():
+            send_forcing(step * few)
+
+        @pl.when(step == 0)
+        def _():
+            pltpu.make_async_copy(
+                forc_out.at[chip_rows(chip)], forc_in.at[core, chip_rows(chip)], forc_recv.at[0]
+            ).start()
+
         @pl.loop(0, NODES // 8)
         def _(i):
             for face in range(2):
@@ -441,7 +496,8 @@
 
     @pl.loop(0, 2 * TILE_GROUPS)
     def _(i):
-        c = lax.rem(i, 2) * TILE_GROUPS + lax.rem(u_me + TILE_GROUPS - i // 2, TILE_GROUPS)
+        on, face = stage(i)
+        c = face * TILE_GROUPS + lax.rem(u_me + on, TILE_GROUPS)
         rows = pl.ds(pl.multiple_of(c * CHUNK, CHUNK), CHUNK)
         q = [
             [dot(place[face, rows, xh * 1024 : (xh + 1) * 1024], dyn[face]) for xh in range(2)]
@@ -449,79 +505,125 @@
         ]
         turn = pltpu.roll(jnp.where(low_row, q[1][0], q[0][1]), 64, 1)
         dyn_out[rows, :] = (jnp.where(low_row, q[0][0], q[1][1]) + turn).astype(jnp.bfloat16)
-        spread(c * group, dyn_out, dyn_in, dyn_recv.at[f * TILE_GROUPS + u_me])
-
-    arrived(forc_in, forc_recv)
+        spread(c, dyn_out, dyn_in, dyn_recv.at[f * TILE_GROUPS + u_me])
+
+    arrived(forc_in.at[core], forc_recv.at[0])
+    sent.append(
+        remote(
+            forc_in.at[core],
+            forc_in.at[core],
+            forc_send.at[1],
+            forc_recv.at[1],
+            at(2 * chip + 1 - core),
+        )
+    )
+    arrived(forc_in.at[1 - core], forc_recv.at[1])
 
     @pl.loop(0, COLUMNS // CHUNK)
     def _(i):
         cols = pl.ds(pl.multiple_of(i * CHUNK, CHUNK), CHUNK)
-        pre[:, cols] += dot(w_in_v[:, CHANNELS : 2 * CHANNELS], forc_in[cols, :], NT)
+        half = CHUNK // 2
+        blocks = []
+        for k in range(0, half, per_peer):
+            rows = pl.ds(pl.multiple_of(i * half + k, 16), per_peer)
+            blocks += [forc_in[0, rows, :], forc_in[1, rows, :]]
+        pre[:, cols] += dot(w_forc[...], jnp.concatenate(blocks, axis=0), NT)
 
     loads[6].wait()
     loads[7].wait()
     level_lane = iota((256, CHANNELS), 1)
     level_row = iota((256, CHANNELS), 0)
 
-    @pl.loop(0, TILE_GROUPS)
-    def _(v):
-        u = lax.rem(u_me + v, TILE_GROUPS)
-        halves = []
-        for h in range(2):
-            c = h * TILE_GROUPS + u
-            rows = pl.ds(pl.multiple_of(c * CHUNK, CHUNK), CHUNK)
-            arrived(dyn_in.at[rows], dyn_recv.at[c])
-            halves.append(dyn_in[rows, :])
-        block = jnp.concatenate(halves, axis=1)
-        for face in range(2):
-            c = face * TILE_GROUPS + u
-            cols = pl.ds(pl.multiple_of(c * CHUNK, CHUNK), CHUNK)
-            hidden = pre[:, cols] + dot(w_dyn[:, face * 256 : (face + 1) * 256], block, NT)
-            hidden = leaky(hidden).astype(jnp.bfloat16)
-            hidden = dot(w_mid_v[...], hidden) + twice(bias_mid[...])
-            hidden = leaky(hidden).astype(jnp.bfloat16)
-            result = dot(w_out_v[...], hidden) + twice(bias_out[...])
-            result = result.astype(jnp.bfloat16)
-            diag_v[:, cols] = result[CHANNELS:, :]
-            row = level_lane // LEVELS * 16 + level_lane % 16
-            row = row + level_lane // HALF % 2 * 128 + face * 64
-            pick = (level_row == row).astype(jnp.bfloat16)
-            change = result[0:CHANNELS, :].astype(jnp.float32).T
-            value = dot(block, pick) + physics_weight * change
-            back_out[cols, :] = value.astype(jnp.bfloat16)
-            spread(c * group, back_out, back_in, back_recv.at[f * TILE_GROUPS + u_me])
+    @pl.loop(0, 2 * TILE_GROUPS)
+    def _(i):
+        on, face = stage(i)
+        u = lax.rem(u_me + on, TILE_GROUPS)
+        chunks = [
+            pl.ds(pl.multiple_of((h * TILE_GROUPS + u) * CHUNK, CHUNK), CHUNK) for h in range(2)
+        ]
+
+        @pl.when((i == 0) | (i == 2) | (i == 3) | (i == 6))
+        def _():
+            for h in range(2):
+                arrived(dyn_in.at[chunks[h]], dyn_recv.at[h * TILE_GROUPS + u])
+
+        block = jnp.concatenate([dyn_in[chunks[0], :], dyn_in[chunks[1], :]], axis=1)
+        c = face * TILE_GROUPS + u
+        cols = pl.ds(pl.multiple_of(c * CHUNK, CHUNK), CHUNK)
+        first = w_dyn[:, pl.ds(pl.multiple_of(face * 256, 256), 256)]
+        hidden = leaky(pre[:, cols] + dot(first, block, NT)).astype(jnp.bfloat16)
+        hidden = dot(w_mid_v[...], hidden) + twice(bias_mid[...])
+        hidden = leaky(hidden).astype(jnp.bfloat16)
+        result = dot(w_out_v[...], hidden) + twice(bias_out[...])
+        result = result.astype(jnp.bfloat16)
+        diag_v[:, cols] = result[CHANNELS:, :]
+        row = level_lane // LEVELS * 16 + level_lane % 16
+        row = row + level_lane // HALF % 2 * 128 + face * 64
+        pick = (level_row == row).astype(jnp.bfloat16)
+        change = result[0:CHANNELS, :].astype(jnp.float32).T
+        value = dot(block, pick) + physics_weight * change
+        back_out[cols, :] = value.astype(jnp.bfloat16)
+        spread(c, back_out, back_in, back_recv.at[f * TILE_GROUPS + u_me])
 
     diag_copy = pltpu.make_async_copy(diag_v, diagnostics, out_sem.at[0])
     diag_copy.start()
 
-    for v in range(TILE_GROUPS):
+    for v in (2, 1, 3, 0):
         u = lax.rem(u_me + TILE_GROUPS - v, TILE_GROUPS)
+        parts = []
         for face in range(2):
             c = face * TILE_GROUPS + u
             rows = pl.ds(pl.multiple_of(c * CHUNK, CHUNK), CHUNK)
             arrived(back_in.at[rows], back_recv.at[c])
-            back = back_in[rows, :]
-            for k in range(0, COLUMNS, 512):
-                value = dot(back, place[f, rows, k : k + 512], TN)
-                if v == 0 and face == 0:
-                    total[:, k : k + 512] = value
-                elif v < TILE_GROUPS - 1 or face == 0:
-                    total[:, k : k + 512] += value
-                else:
-                    value = total[:, k : k + 512] + value
-                    for x in range(4):
-                        updated_v[pl.ds(k // SIZE_Y + x, CHANNELS, stride=SIZE_X), :] = value[
-                            :, x * SIZE_Y : (x + 1) * SIZE_Y
-                        ]
-    updated_copy = pltpu.make_async_copy(updated_v, updated, out_sem.at[1])
+            parts.append((back_in[rows, :], rows))
+        for k in range(0, COLUMNS, 512):
+            value = sum(dot(back, place[f, rows, k : k + 512], TN) for back, rows in parts)
+            value = value.astype(jnp.bfloat16)
+            total[:, k : k + 512] = value if v == 2 else total[:, k : k + 512] + value
+    updated_copy = pltpu.make_async_copy(total, updated, out_sem.at[1])
     updated_copy.start()
     for copy in sent:
         copy.wait_send()
     away = pl.ds(0, (devices - 1) * per_peer)
-    for out in (forc_out, dyn_out, back_out):
+    for out in (dyn_out, back_out):
         arrived(out.at[away], relay_send)
+    arrived(forc_out.at[pl.ds(0, (chips - 1) * per_peer)], forc_send.at[0])
     diag_copy.wait()
     updated_copy.wait()
+
+
+PIECES = 4
+
+
+def finish(new, diag, updated, diagnostics, new_v, diag_v, updated_v, load_sem, out_sem):
+    n, d = CHANNELS // PIECES, (OUT - CHANNELS) // PIECES // 16 * 16
+    cuts = [pl.ds(k * n, n) for k in range(PIECES)]
+    cuts += [pl.ds(k * d, d if k < PIECES - 1 else OUT - CHANNELS - k * d) for k in range(PIECES)]
+    ends = ((new, new_v),) * PIECES + ((diag, diag_v),) * PIECES
+    loads = [
+        pltpu.make_async_copy(src.at[cut], dst.at[cut], load_sem.at[k])
+        for k, (cut, (src, dst)) in enumerate(zip(cuts, ends))
+    ]
+    for copy in loads:
+        copy.start()
+    outs = []
+
+    def out(src, dst):
+        outs.append(pltpu.make_async_copy(src, dst, out_sem.at[len(outs)]))
+        outs[-1].start()
+
+    for k in range(PIECES):
+        loads[k].wait()
+        for x in range(SIZE_X):
+            block = new_v[k * n : (k + 1) * n, x * SIZE_Y : (x + 1) * SIZE_Y]
+            updated_v[pl.ds(k * n * SIZE_X + x, n, stride=SIZE_X), :] = block.astype(jnp.float32)
+        rows = pl.ds(k * n * SIZE_X, n * SIZE_X)
+        out(updated_v.at[rows], updated.at[rows])
+    for k in range(PIECES, 2 * PIECES):
+        loads[k].wait()
+        out(diag_v.at[cuts[k]], diagnostics.at[cuts[k]])
+    for copy in outs:
+        copy.wait()
 
 
 def local(
@@ -550,7 +652,7 @@
         pltpu.VMEM((SIZE_X, SIZE_Y), f32),
         pltpu.VMEM((12 * FORC, SIZE_X, SIZE_Y), b16),
         pltpu.VMEM((AUX, COLUMNS), b16),
-        pltpu.VMEM(w_in.shape, b16),
+        pltpu.VMEM(w_in.shape[::-1], b16),
         pltpu.VMEM(w_mid.shape, b16),
         pltpu.VMEM(w_out.shape, b16),
         dma((8,)),
@@ -571,8 +673,8 @@
         pltpu.VMEM((2, COLUMNS, COLUMNS), b16),
         pltpu.VMEM((48 * SIZE_X, SIZE_Y), f32),
         pltpu.VMEM((128, COLUMNS), b16),
-        pltpu.VMEM((COLUMNS, 128), b16),
-        pltpu.VMEM((COLUMNS, 128), b16),
+        pltpu.VMEM((COLUMNS // 2, 128), b16),
+        pltpu.VMEM((2, COLUMNS // 2, 128), b16),
         pltpu.VMEM((2, COLUMNS // 2, 128), b16),
         pltpu.VMEM((COLUMNS, 128), b16),
         pltpu.VMEM((COLUMNS, 128), b16),
@@ -580,19 +682,20 @@
         pltpu.VMEM((COLUMNS, 128), b16),
         pltpu.VMEM((HIDDEN, COLUMNS), f32),
         pltpu.VMEM((HIDDEN, AUX), b16),
+        pltpu.VMEM((HIDDEN, 128), b16),
         pltpu.VMEM((HIDDEN, 512), b16),
         pltpu.VMEM((HIDDEN, 128), f32),
         pltpu.VMEM((HIDDEN, 128), f32),
         pltpu.VMEM((OUT, 128), f32),
         pltpu.VMEM((OUT - CHANNELS, COLUMNS), b16),
-        pltpu.VMEM((CHANNELS, COLUMNS), f32),
-        pltpu.VMEM((CHANNELS * SIZE_X, SIZE_Y), f32),
+        pltpu.VMEM((CHANNELS, COLUMNS), b16),
         dma((4,)),
         dma((4,)),
         dma((3, 2, 2)),
         dma((3, 2, 2)),
         dma,
-        dma,
+        dma((2,)),
+        dma((2,)),
         dma((2 * TILE_GROUPS,)),
         dma((2 * TILE_GROUPS,)),
         dma((2,)),
@@ -600,7 +703,7 @@
     updated, diagnostics = pl.pallas_call(
         functools.partial(kernel, tiles),
         out_shape=(
-            jax.ShapeDtypeStruct((CHANNELS * SIZE_X, SIZE_Y), f32),
+            jax.ShapeDtypeStruct((CHANNELS, COLUMNS), b16),
             jax.ShapeDtypeStruct((OUT - CHANNELS, COLUMNS), b16),
         ),
         in_specs=[
@@ -631,13 +734,30 @@
         aux_inputs,
         batch_pos,
         day_of_year,
-        w_in,
-        b_in.reshape(1, HIDDEN),
+        w_in.T,
+        b_in,
         w_mid,
-        b_mid.reshape(1, HIDDEN),
+        b_mid,
         w_out,
-        b_out.reshape(1, OUT),
+        b_out,
     )
+    updated, diagnostics = pl.pallas_call(
+        finish,
+        out_shape=(
+            jax.ShapeDtypeStruct((CHANNELS * SIZE_X, SIZE_Y), f32),
+            jax.ShapeDtypeStruct((OUT - CHANNELS, COLUMNS), b16),
+        ),
+        in_specs=[anywhere, anywhere],
+        out_specs=(anywhere, anywhere),
+        scratch_shapes=[
+            pltpu.VMEM((CHANNELS, COLUMNS), b16),
+            pltpu.VMEM((OUT - CHANNELS, COLUMNS), b16),
+            pltpu.VMEM((CHANNELS * SIZE_X, SIZE_Y), f32),
+            dma((2 * PIECES,)),
+            dma((2 * PIECES,)),
+        ],
+        compiler_params=pltpu.CompilerParams(vmem_limit_bytes=60 * 2**20),
+    )(updated, diagnostics)
     return updated.reshape(tracers.shape), diagnostics
 
 

time: 70.7 us -> 58.9 us (0.83)
  local copies, waits for them, and re-layouts: 6.7 us -> 0 us
  Pallas kernels: 62.4 us -> 57.4 us
    pallas_call x1, Pallas kernels: 62.4 us -> 54.9 us  [local(): pl.pallas_call(functools.partial(kernel, tiles), out_shape=(jax.ShapeDtyp...]
    unnamed x5 -> x0, local copies, waits for them, and re-layouts: 5.45 us -> none
    pallas_call x0 -> x1, Pallas kernels: none -> 2.52 us  [local(): pl.pallas_call(finish, out_shape=(jax.ShapeDtypeStruct((CHANNELS * SIZE_X...]
    reshape x1 -> x0, local copies, waits for them, and re-layouts: 1.25 us -> none  [local(): b_out.reshape(1, OUT)]
where the time goes in v1:
time: 58.9 us; the launch traced here: 58.7 us
  Pallas kernels  57.4 us (97%)
  between operations  1.29 us (2%)
    pallas_call x1, Pallas kernels, local(): pl.pallas_call(functools.partial(kernel, tiles), out_shape=(jax.ShapeDtyp...  54.9 us
    pallas_call x1, Pallas kernels, local(): pl.pallas_call(finish, out_shape=(jax.ShapeDtypeStruct((CHANNELS * SIZE_X...  2.52 us

profile of v1, /device:TPU:1, one launch (start us, length us, event | category | flops | bytes accessed | tf_op | source)
XLA Modules:
  0.0 58.7 jit_solution(6767320228221658528)
XLA Ops:
  1.3 54.9 %shard_map.140 = (bf16[128,2048]{1,0:T(8,128)(2,1)}, bf16[240,2048]{1,0:T(8,128)(2,1)}) custom-call(f32[2048,128]{1,0:T(8,128)} %bitcast.6, f32[1024,128]{1,0:T(8,128)} %bitcast.8, f32[16,128]{1,0:T(8,128)} %metric.1, bf16[528,16,128]{2,1,0:T(8,128)(2,1)} %bitcast.5, bf16[384,2048]{1,0:T(8,128)(2,1)} %aux.1, s32[16,128]{1,0:T(8,128)} %batch_pos.1, ...), custom_call_target="tpu_custom_call" | custom-call | tf_op jit(solution)/shard_map/pallas_call | solution.py:703
  56.2 2.5 %shard_map.141 = (f32[2048,128]{1,0:T(8,128)}, bf16[240,2048]{1,0:T(8,128)(2,1)}) custom-call(bf16[128,2048]{1,0:T(8,128)(2,1)} %get-tuple-element.6.new, bf16[240,2048]{1,0:T(8,128)(2,1)} %get-tuple-element.7.diag), custom_call_target="tpu_custom_call" | custom-call | tf_op jit(solution)/shard_map/pallas_call | solution.py:744

commit v2 on v1

--- a/solution.py
+++ b/solution.py
@@ -60,9 +60,7 @@
 
 
 def stage(i):
-    a = (i + 2) // 4
-    pair = a % 2
-    return 2 - a + pair * 2 * (i % 2), pair * ((i + 2) // 2 - 2) + (1 - pair) * (i % 2)
+    return 2 - i + i // 2 * (7 - 2 * i)
 
 
 NT = ((1,), (1,))
@@ -95,7 +93,6 @@
     w_mid_v,
     w_out_v,
     load_sem,
-    half_f32,
     half_b16,
     wind_b16,
     state_in,
@@ -128,6 +125,7 @@
     bias_out,
     diag_v,
     total,
+    known,
     near_send,
     near_recv,
     halo_send,
@@ -175,15 +173,37 @@
     for load in loads:
         load.start()
 
+    def signal(sem, target):
+        pl.semaphore_signal(sem, inc=1, device_id=target, device_id_type=MESH)
+
+    near_tiles = 4
+    middle = min(4, tiles // near_tiles)
+    high = tiles // (near_tiles * middle)
+    t_low, t_middle, t_high = t % near_tiles, t // near_tiles % middle, t // (near_tiles * middle)
+    along_middle = [
+        t + (lax.rem(t_middle + k, middle) - t_middle) * near_tiles for k in range(1, middle)
+    ]
+    along_high = [
+        t + (lax.rem(t_high + k, high) - t_high) * near_tiles * middle for k in range(1, high)
+    ]
+    along_low = [t - t_low + lax.rem(t_low + k, near_tiles) for k in range(near_tiles)]
+    greeted = [(other, tile) for tile in along_low] + [(f, tile) for tile in along_low[1:]]
+    greeted += [(f, tile) for tile in [right, left] + along_middle + along_high]
     barrier = pltpu.get_barrier_semaphore()
-
-    @pl.loop(1, devices)
-    def _(k):
-        p = lax.rem(me + k, devices)
-        pl.semaphore_signal(barrier, inc=1, device_id=at(p), device_id_type=MESH)
-
-    loads[0].wait()
-    for h in range(2):
+    for target in greeted:
+        signal(barrier, target)
+
+    def remote(src, dst, send, recv, target):
+        copy = pltpu.make_async_remote_copy(
+            src, dst, send, recv, device_id=target, device_id_type=MESH
+        )
+        copy.start()
+        return copy
+
+    def arrived(ref, sem):
+        pltpu.make_async_copy(ref, ref, sem).wait()
+
+    def turn_winds(h):
         for g in range(4):
             rows = [
                 winds_v[pl.ds(c * 512 + h * 256 + xh * 8 + 2 * g + lo, HALF, stride=SIZE_X), :]
@@ -192,42 +212,54 @@
                 for xh in range(2)
             ]
             wind_b16[h, g] = jnp.concatenate(rows, axis=0).T.astype(jnp.bfloat16)
+
+    def turn_state(h, x):
+        rows = [
+            tracers_v[pl.ds(i * 512 + h * 256 + xh * 8 + x, HALF, stride=SIZE_X), :]
+            for xh in range(2)
+            for i in range(FIELDS)
+        ]
+        turned = jnp.concatenate(rows, axis=0).T
+        half_b16[h, x] = turned.astype(jnp.bfloat16)
+        return turned
+
+    partner = (other, t)
+    loads[0].wait()
+    turn_winds(other)
     loads[1].wait()
-    for h in range(2):
-        for x in range(8):
-            rows = [
-                tracers_v[pl.ds(i * 512 + h * 256 + xh * 8 + x, HALF, stride=SIZE_X), :]
-                for xh in range(2)
-                for i in range(FIELDS)
-            ]
-            turned = jnp.concatenate(rows, axis=0).T
-            half_f32[h, x] = turned
-            half_b16[h, x] = turned.astype(jnp.bfloat16)
+    turn_state(other, 0)
+    pl.semaphore_wait(barrier, len(greeted))
+    for tile in along_middle:
+        signal(known.at[0], (f, tile))
+    sent = [
+        remote(wind_b16.at[other], wind_in.at[f], near_send.at[2], near_recv.at[2], partner)
+    ]
+    for x in range(8):
+        if x > 0:
+            turn_state(other, x)
+        sent.append(
+            remote(
+                half_b16.at[other, x],
+                state_in.at[f, x],
+                near_send.at[3 + x],
+                near_recv.at[3 + x],
+                partner,
+            )
+        )
     loads[2].wait()
     face_rows = pl.ds(pl.multiple_of(f * SIZE_X, SIZE_X), SIZE_X)
-    metric_all[0, face_rows, :] = metric_v[...]
-    pos_all[f] = batch_pos[...]
-
-    pl.semaphore_wait(barrier, devices - 1)
-
-    def remote(src, dst, send, recv, target):
-        copy = pltpu.make_async_remote_copy(
-            src, dst, send, recv, device_id=target, device_id_type=MESH
-        )
-        copy.start()
-        return copy
-
-    def arrived(ref, sem):
-        pltpu.make_async_copy(ref, ref, sem).wait()
-
-    partner = (other, t)
-    sent = [
+    sent += [
         remote(metric_v, metric_all.at[0, face_rows], near_send.at[0], near_recv.at[0], partner),
         remote(batch_pos, pos_all.at[f], near_send.at[1], near_recv.at[1], partner),
     ]
-    sides = ((0, right, SIZE_Y - HALO), (1, left, 0))
-    for face in range(2):
-        for side, tile, start in sides:
+    metric_all[0, face_rows, :] = metric_v[...]
+    pos_all[f] = batch_pos[...]
+    turn_winds(f)
+    for x in range(8):
+        state[f, x, 0:SIZE_Y, :] = turn_state(f, x)
+
+    def send_halo(face):
+        for side, tile, start in ((0, right, SIZE_Y - HALO), (1, left, 0)):
             rows = pl.ds(start, HALO)
             for kind, src, dst in (
                 (0, metric_v, metric_all.at[1 + side, face_rows]),
@@ -243,23 +275,34 @@
                         (face, tile),
                     )
                 )
-    sent.append(remote(wind_b16.at[other], wind_in.at[f], near_send.at[2], near_recv.at[2], partner))
-    sent.append(remote(half_b16.at[other], state_in.at[f], near_send.at[3], near_recv.at[3], partner))
+
+    if middle > 1:
+        pl.semaphore_wait(known.at[0], middle - 1)
+    for tile in along_high:
+        signal(known.at[1], (f, tile))
+    send_halo(f)
 
     def fill_place(face):
         pos = pos_all[face]
         slot = pos // COLUMNS * per_peer + pos % per_peer
+        one = jnp.ones((CHUNK, SIZE_Y), jnp.bfloat16)
+        zero = jnp.zeros((CHUNK, SIZE_Y), jnp.bfloat16)
 
         @pl.loop(0, COLUMNS // CHUNK)
         def _(i):
             rows = pl.ds(pl.multiple_of(i * CHUNK, CHUNK), CHUNK)
-            index = iota((CHUNK, SIZE_Y), 0)
+            index = iota((CHUNK, SIZE_Y), 0).astype(jnp.int16)
             here = slot - i * CHUNK
             for x in range(SIZE_X):
-                hit = index == here[x : x + 1, :]
-                place[face, rows, x * SIZE_Y : (x + 1) * SIZE_Y] = hit.astype(jnp.bfloat16)
+                row = jnp.broadcast_to(here[x : x + 1, :], (16, SIZE_Y)).astype(jnp.int16)
+                row = jnp.concatenate([row] * (CHUNK // 16), axis=0)
+                hit = jnp.where(index == row, one, zero)
+                place[face, rows, x * SIZE_Y : (x + 1) * SIZE_Y] = hit
 
     fill_place(f)
+    if high > 1:
+        pl.semaphore_wait(known.at[1], high - 1)
+    send_halo(other)
 
     loads[5].wait()
     months = day[0] * 12
@@ -355,13 +398,16 @@
     w_dyn[...] = dot(w_in_v[0:CHANNELS, :], pick.astype(jnp.bfloat16), TN).astype(jnp.bfloat16)
     loads[4].wait()
 
-    def twice(value):
-        return jnp.concatenate([value, value], axis=1)
+    def twice(one, two=None):
+        return jnp.concatenate([one, one if two is None else two], axis=1)
 
     @pl.loop(0, COLUMNS // CHUNK)
     def _(i):
         cols = pl.ds(pl.multiple_of(i * CHUNK, CHUNK), CHUNK)
         pre[:, cols] = dot(w_aux[...], aux_v[:, cols]) + twice(bias_in[...])
+
+    arrived(pos_all.at[0], near_recv.at[1])
+    fill_place(other)
 
     arrived(metric_all.at[0, pl.ds(0, SIZE_X)], near_recv.at[0])
     for face in range(2):
@@ -393,11 +439,7 @@
                 two = jnp.broadcast_to(value[:, k + 8 : k + 9], (WIDE, 128))
                 into[face, x] = jnp.where(low, one, two)
 
-    arrived(pos_all.at[0], near_recv.at[1])
-    fill_place(other)
-
     wind_in[f] = wind_b16[f]
-    state[f, :, 0:SIZE_Y, :] = half_f32[f]
     out_lane = iota((128, 512), 1)
     from_lane = out_lane // 128 * 32 + out_lane // 64 % 2 * 16 + out_lane % 16
     widen = (iota((128, 512), 0) == from_lane).astype(jnp.bfloat16)
@@ -421,20 +463,24 @@
     for face in range(2):
         state[face, :, SIZE_Y : SIZE_Y + HALO, :] = halo_state[1, face].astype(jnp.float32)
         state[face, :, SIZE_Y + HALO :, :] = halo_state[0, face].astype(jnp.float32)
-    arrived(state_in.at[0], near_recv.at[3])
-    state[other, :, 0:SIZE_Y, :] = state_in[other].astype(jnp.float32)
+    for x in range(8):
+        arrived(state_in.at[0, x], near_recv.at[3 + x])
+        state[other, x, 0:SIZE_Y, :] = state_in[other, x].astype(jnp.float32)
 
     low_half = iota((NODES, 128), 1) < 64
 
     @pl.loop(0, SUBSTEPS)
     def _(step):
-        few = chips // SUBSTEPS
-        for k in range(1, few):
-            send_forcing(step * few + k)
-
-        @pl.when(step > 0)
+        few = chips // 2
+
+        @pl.when(step < 2)
         def _():
-            send_forcing(step * few)
+            for k in range(1, few):
+                send_forcing(step * few + k)
+
+        @pl.when(step == 1)
+        def _():
+            send_forcing(few)
 
         @pl.when(step == 0)
         def _():
@@ -492,20 +538,30 @@
                 jnp.bfloat16
             )
 
-    low_row = iota((CHUNK, 128), 1) < 64
-
-    @pl.loop(0, 2 * TILE_GROUPS)
+    low_row = iota((2 * CHUNK, 128), 1) < 64
+
+    @pl.loop(0, TILE_GROUPS)
     def _(i):
-        on, face = stage(i)
-        c = face * TILE_GROUPS + lax.rem(u_me + on, TILE_GROUPS)
-        rows = pl.ds(pl.multiple_of(c * CHUNK, CHUNK), CHUNK)
+        u = lax.rem(u_me + stage(i), TILE_GROUPS)
+        chunks = [(other * TILE_GROUPS + u), (f * TILE_GROUPS + u)]
+        rows = [pl.ds(pl.multiple_of(c * CHUNK, CHUNK), CHUNK) for c in chunks]
         q = [
-            [dot(place[face, rows, xh * 1024 : (xh + 1) * 1024], dyn[face]) for xh in range(2)]
+            [
+                dot(
+                    jnp.concatenate(
+                        [place[face, r, xh * 1024 : (xh + 1) * 1024] for r in rows], axis=0
+                    ),
+                    dyn[face],
+                )
+                for xh in range(2)
+            ]
             for face in range(2)
         ]
         turn = pltpu.roll(jnp.where(low_row, q[1][0], q[0][1]), 64, 1)
-        dyn_out[rows, :] = (jnp.where(low_row, q[0][0], q[1][1]) + turn).astype(jnp.bfloat16)
-        spread(c, dyn_out, dyn_in, dyn_recv.at[f * TILE_GROUPS + u_me])
+        packed = (jnp.where(low_row, q[0][0], q[1][1]) + turn).astype(jnp.bfloat16)
+        for k in range(2):
+            dyn_out[rows[k], :] = packed[k * CHUNK : (k + 1) * CHUNK, :]
+            spread(chunks[k], dyn_out, dyn_in, dyn_recv.at[f * TILE_GROUPS + u_me])
 
     arrived(forc_in.at[core], forc_recv.at[0])
     sent.append(
@@ -534,36 +590,36 @@
     level_lane = iota((256, CHANNELS), 1)
     level_row = iota((256, CHANNELS), 0)
 
-    @pl.loop(0, 2 * TILE_GROUPS)
+    @pl.loop(0, TILE_GROUPS)
     def _(i):
-        on, face = stage(i)
-        u = lax.rem(u_me + on, TILE_GROUPS)
+        u = lax.rem(u_me + stage(i), TILE_GROUPS)
         chunks = [
             pl.ds(pl.multiple_of((h * TILE_GROUPS + u) * CHUNK, CHUNK), CHUNK) for h in range(2)
         ]
-
-        @pl.when((i == 0) | (i == 2) | (i == 3) | (i == 6))
-        def _():
-            for h in range(2):
-                arrived(dyn_in.at[chunks[h]], dyn_recv.at[h * TILE_GROUPS + u])
-
+        for h in range(2):
+            arrived(dyn_in.at[chunks[h]], dyn_recv.at[h * TILE_GROUPS + u])
         block = jnp.concatenate([dyn_in[chunks[0], :], dyn_in[chunks[1], :]], axis=1)
-        c = face * TILE_GROUPS + u
-        cols = pl.ds(pl.multiple_of(c * CHUNK, CHUNK), CHUNK)
-        first = w_dyn[:, pl.ds(pl.multiple_of(face * 256, 256), 256)]
-        hidden = leaky(pre[:, cols] + dot(first, block, NT)).astype(jnp.bfloat16)
-        hidden = dot(w_mid_v[...], hidden) + twice(bias_mid[...])
-        hidden = leaky(hidden).astype(jnp.bfloat16)
-        result = dot(w_out_v[...], hidden) + twice(bias_out[...])
+        turned = block.T
+        hidden = [
+            leaky(pre[:, chunks[face]] + dot(w_dyn[:, face * 256 : (face + 1) * 256], turned))
+            for face in range(2)
+        ]
+        hidden = twice(*hidden).astype(jnp.bfloat16)
+        hidden = leaky(dot(w_mid_v[...], hidden) + twice(twice(bias_mid[...])))
+        result = dot(w_out_v[...], hidden.astype(jnp.bfloat16)) + twice(twice(bias_out[...]))
         result = result.astype(jnp.bfloat16)
-        diag_v[:, cols] = result[CHANNELS:, :]
-        row = level_lane // LEVELS * 16 + level_lane % 16
-        row = row + level_lane // HALF % 2 * 128 + face * 64
-        pick = (level_row == row).astype(jnp.bfloat16)
-        change = result[0:CHANNELS, :].astype(jnp.float32).T
-        value = dot(block, pick) + physics_weight * change
-        back_out[cols, :] = value.astype(jnp.bfloat16)
-        spread(c, back_out, back_in, back_recv.at[f * TILE_GROUPS + u_me])
+        for face in range(2):
+            part = result[:, face * CHUNK : (face + 1) * CHUNK]
+            diag_v[:, chunks[face]] = part[CHANNELS:, :]
+            row = level_lane // LEVELS * 16 + level_lane % 16
+            row = row + level_lane // HALF % 2 * 128 + face * 64
+            pick = (level_row == row).astype(jnp.bfloat16)
+            change = part[0:CHANNELS, :].astype(jnp.float32).T
+            value = dot(block, pick) + physics_weight * change
+            back_out[chunks[face], :] = value.astype(jnp.bfloat16)
+        for face in (other, f):
+            c = face * TILE_GROUPS + u
+            spread(c, back_out, back_in, back_recv.at[f * TILE_GROUPS + u_me])
 
     diag_copy = pltpu.make_async_copy(diag_v, diagnostics, out_sem.at[0])
     diag_copy.start()
@@ -656,7 +712,6 @@
         pltpu.VMEM(w_mid.shape, b16),
         pltpu.VMEM(w_out.shape, b16),
         dma((8,)),
-        pltpu.VMEM((2, 8, SIZE_Y, 128), f32),
         pltpu.VMEM((2, 8, SIZE_Y, 128), b16),
         pltpu.VMEM((2, 4, SIZE_Y, 128), b16),
         pltpu.VMEM((2, 8, SIZE_Y, 128), b16),
@@ -689,8 +744,9 @@
         pltpu.VMEM((OUT, 128), f32),
         pltpu.VMEM((OUT - CHANNELS, COLUMNS), b16),
         pltpu.VMEM((CHANNELS, COLUMNS), b16),
-        dma((4,)),
-        dma((4,)),
+        pltpu.SemaphoreType.REGULAR((2,)),
+        dma((11,)),
+        dma((11,)),
         dma((3, 2, 2)),
         dma((3, 2, 2)),
         dma,

time: 58.9 us -> 57.4 us (0.975)
  Pallas kernels: 57.4 us -> 55.9 us
    pallas_call x1, Pallas kernels: 54.9 us -> 53.4 us  [local(): pl.pallas_call(functools.partial(kernel, tiles), out_shape=(jax.ShapeDtyp...]
where the time goes in v2:
time: 57.4 us; the launch traced here: 57.2 us
  Pallas kernels  55.9 us (97%)
  between operations  1.29 us (2%)
    pallas_call x1, Pallas kernels, local(): pl.pallas_call(functools.partial(kernel, tiles), out_shape=(jax.ShapeDtyp...  53.4 us
    pallas_call x1, Pallas kernels, local(): pl.pallas_call(finish, out_shape=(jax.ShapeDtypeStruct((CHANNELS * SIZE_X...  2.52 us

profile of v2, /device:TPU:1, one launch (start us, length us, event | category | flops | bytes accessed | tf_op | source)
XLA Modules:
  0.0 57.2 jit_solution(3739429115832258164)
XLA Ops:
  1.3 53.4 %shard_map.140 = (bf16[128,2048]{1,0:T(8,128)(2,1)}, bf16[240,2048]{1,0:T(8,128)(2,1)}) custom-call(f32[2048,128]{1,0:T(8,128)} %bitcast.6, f32[1024,128]{1,0:T(8,128)} %bitcast.8, f32[16,128]{1,0:T(8,128)} %metric.1, bf16[528,16,128]{2,1,0:T(8,128)(2,1)} %bitcast.5, bf16[384,2048]{1,0:T(8,128)(2,1)} %aux.1, s32[16,128]{1,0:T(8,128)} %batch_pos.1, ...), custom_call_target="tpu_custom_call" | custom-call | tf_op jit(solution)/shard_map/pallas_call | solution.py:759
  54.7 2.5 %shard_map.141 = (f32[2048,128]{1,0:T(8,128)}, bf16[240,2048]{1,0:T(8,128)(2,1)}) custom-call(bf16[128,2048]{1,0:T(8,128)(2,1)} %get-tuple-element.6.new, bf16[240,2048]{1,0:T(8,128)(2,1)} %get-tuple-element.7.diag), custom_call_target="tpu_custom_call" | custom-call | tf_op jit(solution)/shard_map/pallas_call | solution.py:800

commit v3 on v2

--- a/solution.py
+++ b/solution.py
@@ -60,7 +60,9 @@
 
 
 def stage(i):
-    return 2 - i + i // 2 * (7 - 2 * i)
+    a = (i + 1) // 2
+    pair = a % 2
+    return (2 - a, 1 - pair * (i - 1)), (2 - a + 2 * pair, pair * (2 - i))
 
 
 NT = ((1,), (1,))
@@ -92,6 +94,11 @@
     w_in_v,
     w_mid_v,
     w_out_v,
+    pos_v,
+    day_v,
+    b_in_v,
+    b_mid_v,
+    b_out_v,
     load_sem,
     half_b16,
     wind_b16,
@@ -167,6 +174,11 @@
                 (forcing, forcing_v),
                 (w_mid, w_mid_v),
                 (w_out, w_out_v),
+                (batch_pos, pos_v),
+                (day, day_v),
+                (b_in, b_in_v),
+                (b_mid, b_mid_v),
+                (b_out, b_out_v),
             )
         )
     ]
@@ -247,13 +259,14 @@
             )
         )
     loads[2].wait()
+    loads[8].wait()
     face_rows = pl.ds(pl.multiple_of(f * SIZE_X, SIZE_X), SIZE_X)
     sent += [
         remote(metric_v, metric_all.at[0, face_rows], near_send.at[0], near_recv.at[0], partner),
-        remote(batch_pos, pos_all.at[f], near_send.at[1], near_recv.at[1], partner),
+        remote(pos_v, pos_all.at[f], near_send.at[1], near_recv.at[1], partner),
     ]
     metric_all[0, face_rows, :] = metric_v[...]
-    pos_all[f] = batch_pos[...]
+    pos_all[f] = pos_v[...]
     turn_winds(f)
     for x in range(8):
         state[f, x, 0:SIZE_Y, :] = turn_state(f, x)
@@ -305,7 +318,8 @@
     send_halo(other)
 
     loads[5].wait()
-    months = day[0] * 12
+    loads[9].wait()
+    months = day_v[0] * 12
     month_lo = months // 365
     month_hi = lax.rem(month_lo + 1, 12)
     part = jnp.full((1, 1, SIZE_Y), months - month_lo * 365, jnp.int32).astype(jnp.float32) / 365.0
@@ -322,9 +336,14 @@
     for k in (48, 112):
         forc_mat[k : k + 16, :] = jnp.zeros((16, COLUMNS), jnp.bfloat16)
 
-    def spread(c, out, dst, recv):
-        def send(k):
-            p = c * group + lax.rem(k_me + k, group)
+    low_size = min(near_tiles, group)
+    z_size = group // low_size
+    z_me = k_me // low_size
+    far_first = sorted(range(group), key=lambda k: -min(k // low_size, z_size - k // low_size))
+
+    def spread(i, pair, out, dst, recv):
+        def send(c, k):
+            p = c * group + (z_me + k // low_size) % z_size * low_size + (k_me + k) % low_size
             pltpu.make_async_remote_copy(
                 out.at[own_rows(p)],
                 dst.at[own_rows(me)],
@@ -334,18 +353,29 @@
                 device_id_type=MESH,
             ).start()
 
-        own = c == f * TILE_GROUPS + u_me
-
-        @pl.when(own)
+        @pl.when(i == TILE_GROUPS - 1)
         def _():
-            for k in range(1, group):
-                send(k)
+            for k in far_first:
+                send(pair[0], k)
+                if k > 0:
+                    send(pair[1], k)
             pltpu.make_async_copy(out.at[own_rows(me)], dst.at[own_rows(me)], recv).start()
 
-        @pl.when(jnp.logical_not(own))
+        @pl.when(i < TILE_GROUPS - 1)
         def _():
-            for k in range(group):
-                send(k)
+            for k in far_first:
+                for c in pair:
+                    send(c, k)
+
+    def chunks_of(i):
+        found = []
+        for on, away in stage(i):
+            face, u = lax.rem(f + away, 2), lax.rem(u_me + on, TILE_GROUPS)
+            found.append((face * TILE_GROUPS + u, face, u))
+        return found
+
+    def chunk_rows(c):
+        return pl.ds(pl.multiple_of(c * CHUNK, CHUNK), CHUNK)
 
     chips = devices // 2
     core = lax.rem(t, 2)
@@ -382,9 +412,11 @@
             n = min(128, size - k)
             into[k : k + n, :] = jnp.broadcast_to(ref[k : k + n].reshape(1, n), (128, n)).T
 
-    spread_bias(b_in, bias_in, HIDDEN)
-    spread_bias(b_mid, bias_mid, HIDDEN)
-    spread_bias(b_out, bias_out, OUT)
+    for load in loads[10:]:
+        load.wait()
+    spread_bias(b_in_v, bias_in, HIDDEN)
+    spread_bias(b_mid_v, bias_mid, HIDDEN)
+    spread_bias(b_out_v, bias_out, OUT)
     loads[3].wait()
     w_aux[...] = w_in_v[CHANNELS + FORC :, :].T
     row = iota((CHANNELS, 128), 0)
@@ -542,9 +574,8 @@
 
     @pl.loop(0, TILE_GROUPS)
     def _(i):
-        u = lax.rem(u_me + stage(i), TILE_GROUPS)
-        chunks = [(other * TILE_GROUPS + u), (f * TILE_GROUPS + u)]
-        rows = [pl.ds(pl.multiple_of(c * CHUNK, CHUNK), CHUNK) for c in chunks]
+        chunks = [c for c, _, _ in chunks_of(i)]
+        rows = [chunk_rows(c) for c in chunks]
         q = [
             [
                 dot(
@@ -561,7 +592,7 @@
         packed = (jnp.where(low_row, q[0][0], q[1][1]) + turn).astype(jnp.bfloat16)
         for k in range(2):
             dyn_out[rows[k], :] = packed[k * CHUNK : (k + 1) * CHUNK, :]
-            spread(chunks[k], dyn_out, dyn_in, dyn_recv.at[f * TILE_GROUPS + u_me])
+        spread(i, chunks, dyn_out, dyn_in, dyn_recv.at[f * TILE_GROUPS + u_me])
 
     arrived(forc_in.at[core], forc_recv.at[0])
     sent.append(
@@ -592,34 +623,42 @@
 
     @pl.loop(0, TILE_GROUPS)
     def _(i):
-        u = lax.rem(u_me + stage(i), TILE_GROUPS)
-        chunks = [
-            pl.ds(pl.multiple_of((h * TILE_GROUPS + u) * CHUNK, CHUNK), CHUNK) for h in range(2)
-        ]
-        for h in range(2):
-            arrived(dyn_in.at[chunks[h]], dyn_recv.at[h * TILE_GROUPS + u])
-        block = jnp.concatenate([dyn_in[chunks[0], :], dyn_in[chunks[1], :]], axis=1)
-        turned = block.T
-        hidden = [
-            leaky(pre[:, chunks[face]] + dot(w_dyn[:, face * 256 : (face + 1) * 256], turned))
-            for face in range(2)
-        ]
+        steps = chunks_of(i)
+
+        def arrive(u):
+            for h in range(2):
+                c = h * TILE_GROUPS + u
+                arrived(dyn_in.at[chunk_rows(c)], dyn_recv.at[c])
+
+        @pl.when(i != 2)
+        def _():
+            arrive(steps[0][2])
+
+        @pl.when(i == 1)
+        def _():
+            arrive(steps[1][2])
+
+        blocks, hidden = [], []
+        for c, face, u in steps:
+            halves = [dyn_in[chunk_rows(h * TILE_GROUPS + u), :] for h in range(2)]
+            blocks.append(twice(*halves))
+            first = w_dyn[:, pl.ds(pl.multiple_of(face * 256, 256), 256)]
+            hidden.append(leaky(pre[:, chunk_rows(c)] + dot(first, blocks[-1].T)))
         hidden = twice(*hidden).astype(jnp.bfloat16)
         hidden = leaky(dot(w_mid_v[...], hidden) + twice(twice(bias_mid[...])))
         result = dot(w_out_v[...], hidden.astype(jnp.bfloat16)) + twice(twice(bias_out[...]))
         result = result.astype(jnp.bfloat16)
-        for face in range(2):
-            part = result[:, face * CHUNK : (face + 1) * CHUNK]
-            diag_v[:, chunks[face]] = part[CHANNELS:, :]
+        for k, (c, face, u) in enumerate(steps):
+            part = result[:, k * CHUNK : (k + 1) * CHUNK]
+            diag_v[:, chunk_rows(c)] = part[CHANNELS:, :]
             row = level_lane // LEVELS * 16 + level_lane % 16
             row = row + level_lane // HALF % 2 * 128 + face * 64
             pick = (level_row == row).astype(jnp.bfloat16)
             change = part[0:CHANNELS, :].astype(jnp.float32).T
-            value = dot(block, pick) + physics_weight * change
-            back_out[chunks[face], :] = value.astype(jnp.bfloat16)
-        for face in (other, f):
-            c = face * TILE_GROUPS + u
-            spread(c, back_out, back_in, back_recv.at[f * TILE_GROUPS + u_me])
+            value = dot(blocks[k], pick) + physics_weight * change
+            back_out[chunk_rows(c), :] = value.astype(jnp.bfloat16)
+        pair = [c for c, _, _ in steps]
+        spread(i, pair, back_out, back_in, back_recv.at[f * TILE_GROUPS + u_me])
 
     diag_copy = pltpu.make_async_copy(diag_v, diagnostics, out_sem.at[0])
     diag_copy.start()
@@ -699,7 +738,6 @@
 ):
     tiles = lax.axis_size("tile")
     anywhere = pl.BlockSpec(memory_space=pl.ANY)
-    vmem = pl.BlockSpec(memory_space=pltpu.VMEM)
     f32, b16 = jnp.float32, jnp.bfloat16
     dma = pltpu.SemaphoreType.DMA
     scratch = [
@@ -711,7 +749,12 @@
         pltpu.VMEM(w_in.shape[::-1], b16),
         pltpu.VMEM(w_mid.shape, b16),
         pltpu.VMEM(w_out.shape, b16),
-        dma((8,)),
+        pltpu.VMEM((SIZE_X, SIZE_Y), jnp.int32),
+        pltpu.SMEM((1,), jnp.int32),
+        pltpu.VMEM((HIDDEN,), f32),
+        pltpu.VMEM((HIDDEN,), f32),
+        pltpu.VMEM((OUT,), f32),
+        dma((13,)),
         pltpu.VMEM((2, 8, SIZE_Y, 128), b16),
         pltpu.VMEM((2, 4, SIZE_Y, 128), b16),
         pltpu.VMEM((2, 8, SIZE_Y, 128), b16),
@@ -762,21 +805,7 @@
             jax.ShapeDtypeStruct((CHANNELS, COLUMNS), b16),
             jax.ShapeDtypeStruct((OUT - CHANNELS, COLUMNS), b16),
         ),
-        in_specs=[
-            anywhere,
-            anywhere,
-            anywhere,
-            anywhere,
-            anywhere,
-            vmem,
-            pl.BlockSpec(memory_space=pltpu.SMEM),
-            anywhere,
-            vmem,
-            anywhere,
-            vmem,
-            anywhere,
-            vmem,
-        ],
+        in_specs=[anywhere] * 13,
         out_specs=(anywhere, anywhere),
         scratch_shapes=scratch,
         compiler_params=pltpu.CompilerParams(

time: 57.4 us -> 56.2 us (0.979)
  Pallas kernels: 55.9 us -> 54.8 us
    pallas_call x1, Pallas kernels: 53.4 us -> 52.2 us  [local(): pl.pallas_call(functools.partial(kernel, tiles), out_shape=(jax.ShapeDtyp...]
where the time goes in v3:
time: 56.2 us; the launch traced here: 56 us
  Pallas kernels  54.8 us (98%)
  between operations  1.29 us (2%)
    pallas_call x1, Pallas kernels, local(): pl.pallas_call(functools.partial(kernel, tiles), out_shape=(jax.ShapeDtyp...  52.2 us
    pallas_call x1, Pallas kernels, local(): pl.pallas_call(finish, out_shape=(jax.ShapeDtypeStruct((CHANNELS * SIZE_X...  2.52 us

profile of v3, /device:TPU:1, one launch (start us, length us, event | category | flops | bytes accessed | tf_op | source)
XLA Modules:
  0.0 56.0 jit_solution(11434896778070990078)
XLA Ops:
  1.3 52.2 %shard_map.140 = (bf16[128,2048]{1,0:T(8,128)(2,1)}, bf16[240,2048]{1,0:T(8,128)(2,1)}) custom-call(f32[2048,128]{1,0:T(8,128)} %bitcast.6, f32[1024,128]{1,0:T(8,128)} %bitcast.8, f32[16,128]{1,0:T(8,128)} %metric.1, bf16[528,16,128]{2,1,0:T(8,128)(2,1)} %bitcast.5, bf16[384,2048]{1,0:T(8,128)(2,1)} %aux.1, s32[16,128]{1,0:T(8,128)} %batch_pos.1, ...), custom_call_target="tpu_custom_call" | custom-call | tf_op jit(solution)/shard_map/pallas_call | solution.py:802
  53.5 2.5 %shard_map.141 = (f32[2048,128]{1,0:T(8,128)}, bf16[240,2048]{1,0:T(8,128)(2,1)}) custom-call(bf16[128,2048]{1,0:T(8,128)(2,1)} %get-tuple-element.6.new, bf16[240,2048]{1,0:T(8,128)(2,1)} %get-tuple-element.7.diag), custom_call_target="tpu_custom_call" | custom-call | tf_op jit(solution)/shard_map/pallas_call | solution.py:829

commit v4 on v3

--- a/solution.py
+++ b/solution.py
@@ -503,16 +503,10 @@
 
     @pl.loop(0, SUBSTEPS)
     def _(step):
-        few = chips // 2
-
-        @pl.when(step < 2)
+        @pl.when(step == 0)
         def _():
-            for k in range(1, few):
-                send_forcing(step * few + k)
-
-        @pl.when(step == 1)
-        def _():
-            send_forcing(few)
+            for k in range(1, chips):
+                send_forcing(k)
 
         @pl.when(step == 0)
         def _():
@@ -574,6 +568,17 @@
 
     @pl.loop(0, TILE_GROUPS)
     def _(i):
+        @pl.when(i == TILE_GROUPS - 2)
+        def _():
+            arrived(forc_in.at[core], forc_recv.at[0])
+            remote(
+                forc_in.at[core],
+                forc_in.at[core],
+                forc_send.at[1],
+                forc_recv.at[1],
+                at(2 * chip + 1 - core),
+            )
+
         chunks = [c for c, _, _ in chunks_of(i)]
         rows = [chunk_rows(c) for c in chunks]
         q = [
@@ -594,22 +599,12 @@
             dyn_out[rows[k], :] = packed[k * CHUNK : (k + 1) * CHUNK, :]
         spread(i, chunks, dyn_out, dyn_in, dyn_recv.at[f * TILE_GROUPS + u_me])
 
-    arrived(forc_in.at[core], forc_recv.at[0])
-    sent.append(
-        remote(
-            forc_in.at[core],
-            forc_in.at[core],
-            forc_send.at[1],
-            forc_recv.at[1],
-            at(2 * chip + 1 - core),
-        )
-    )
     arrived(forc_in.at[1 - core], forc_recv.at[1])
 
-    @pl.loop(0, COLUMNS // CHUNK)
+    @pl.loop(0, COLUMNS // CHUNK // 2)
     def _(i):
-        cols = pl.ds(pl.multiple_of(i * CHUNK, CHUNK), CHUNK)
-        half = CHUNK // 2
+        cols = pl.ds(pl.multiple_of(i * 2 * CHUNK, 2 * CHUNK), 2 * CHUNK)
+        half = CHUNK
         blocks = []
         for k in range(0, half, per_peer):
             rows = pl.ds(pl.multiple_of(i * half + k, 16), per_peer)
@@ -683,6 +678,7 @@
     for out in (dyn_out, back_out):
         arrived(out.at[away], relay_send)
     arrived(forc_out.at[pl.ds(0, (chips - 1) * per_peer)], forc_send.at[0])
+    arrived(forc_in.at[core], forc_send.at[1])
     diag_copy.wait()
     updated_copy.wait()
 

time: 56.2 us -> 54.8 us (0.975)
  Pallas kernels: 54.8 us -> 53.3 us
    pallas_call x1, Pallas kernels: 52.2 us -> 50.8 us  [local(): pl.pallas_call(functools.partial(kernel, tiles), out_shape=(jax.ShapeDtyp...]
where the time goes in v4:
time: 54.8 us; the launch traced here: 54.6 us
  Pallas kernels  53.3 us (97%)
  between operations  1.29 us (2%)
    pallas_call x1, Pallas kernels, local(): pl.pallas_call(functools.partial(kernel, tiles), out_shape=(jax.ShapeDtyp...  50.8 us
    pallas_call x1, Pallas kernels, local(): pl.pallas_call(finish, out_shape=(jax.ShapeDtypeStruct((CHANNELS * SIZE_X...  2.52 us

profile of v4, /device:TPU:1, one launch (start us, length us, event | category | flops | bytes accessed | tf_op | source)
XLA Modules:
  0.0 54.6 jit_solution(1501558221256087817)
XLA Ops:
  1.3 50.8 %shard_map.140 = (bf16[128,2048]{1,0:T(8,128)(2,1)}, bf16[240,2048]{1,0:T(8,128)(2,1)}) custom-call(f32[2048,128]{1,0:T(8,128)} %bitcast.6, f32[1024,128]{1,0:T(8,128)} %bitcast.8, f32[16,128]{1,0:T(8,128)} %metric.1, bf16[528,16,128]{2,1,0:T(8,128)(2,1)} %bitcast.5, bf16[384,2048]{1,0:T(8,128)(2,1)} %aux.1, s32[16,128]{1,0:T(8,128)} %batch_pos.1, ...), custom_call_target="tpu_custom_call" | custom-call | tf_op jit(solution)/shard_map/pallas_call | solution.py:798
  52.1 2.5 %shard_map.141 = (f32[2048,128]{1,0:T(8,128)}, bf16[240,2048]{1,0:T(8,128)(2,1)}) custom-call(bf16[128,2048]{1,0:T(8,128)(2,1)} %get-tuple-element.6.new, bf16[240,2048]{1,0:T(8,128)(2,1)} %get-tuple-element.7.diag), custom_call_target="tpu_custom_call" | custom-call | tf_op jit(solution)/shard_map/pallas_call | solution.py:825

commit v5 on v4

--- a/solution.py
+++ b/solution.py
@@ -48,7 +48,7 @@
 
 
 def leaky(value):
-    return jnp.where(value > 0, value, leak_slope * value)
+    return jnp.maximum(value, leak_slope * value)
 
 
 def iota(shape, dim):
@@ -658,6 +658,7 @@
     diag_copy = pltpu.make_async_copy(diag_v, diagnostics, out_sem.at[0])
     diag_copy.start()
 
+    updated_copies = []
     for v in (2, 1, 3, 0):
         u = lax.rem(u_me + TILE_GROUPS - v, TILE_GROUPS)
         parts = []
@@ -670,8 +671,14 @@
             value = sum(dot(back, place[f, rows, k : k + 512], TN) for back, rows in parts)
             value = value.astype(jnp.bfloat16)
             total[:, k : k + 512] = value if v == 2 else total[:, k : k + 512] + value
-    updated_copy = pltpu.make_async_copy(total, updated, out_sem.at[1])
-    updated_copy.start()
+            if v == 0:
+                cols = pl.ds(k, 512)
+                updated_copies.append(
+                    pltpu.make_async_copy(
+                        total.at[:, cols], updated.at[:, cols], out_sem.at[1 + k // 512]
+                    )
+                )
+                updated_copies[-1].start()
     for copy in sent:
         copy.wait_send()
     away = pl.ds(0, (devices - 1) * per_peer)
@@ -680,7 +687,8 @@
     arrived(forc_out.at[pl.ds(0, (chips - 1) * per_peer)], forc_send.at[0])
     arrived(forc_in.at[core], forc_send.at[1])
     diag_copy.wait()
-    updated_copy.wait()
+    for copy in updated_copies:
+        copy.wait()
 
 
 PIECES = 4
@@ -793,7 +801,7 @@
         dma((2,)),
         dma((2 * TILE_GROUPS,)),
         dma((2 * TILE_GROUPS,)),
-        dma((2,)),
+        dma((5,)),
     ]
     updated, diagnostics = pl.pallas_call(
         functools.partial(kernel, tiles),

time: 54.8 us -> 54.6 us (level)
  no operation moved by 1% of the time
where the time goes in v5:
time: 54.6 us; the launch traced here: 54.5 us
  Pallas kernels  53.2 us (97%)
  between operations  1.29 us (2%)
    pallas_call x1, Pallas kernels, local(): pl.pallas_call(functools.partial(kernel, tiles), out_shape=(jax.ShapeDtyp...  50.7 us
    pallas_call x1, Pallas kernels, local(): pl.pallas_call(finish, out_shape=(jax.ShapeDtypeStruct((CHANNELS * SIZE_X...  2.52 us

profile of v5, /device:TPU:1, one launch (start us, length us, event | category | flops | bytes accessed | tf_op | source)
XLA Modules:
  0.0 54.5 jit_solution(9431808058053662537)
XLA Ops:
  1.3 50.7 %shard_map.140 = (bf16[128,2048]{1,0:T(8,128)(2,1)}, bf16[240,2048]{1,0:T(8,128)(2,1)}) custom-call(f32[2048,128]{1,0:T(8,128)} %bitcast.6, f32[1024,128]{1,0:T(8,128)} %bitcast.8, f32[16,128]{1,0:T(8,128)} %metric.1, bf16[528,16,128]{2,1,0:T(8,128)(2,1)} %bitcast.5, bf16[384,2048]{1,0:T(8,128)(2,1)} %aux.1, s32[16,128]{1,0:T(8,128)} %batch_pos.1, ...), custom_call_target="tpu_custom_call" | custom-call | tf_op jit(solution)/shard_map/pallas_call | solution.py:806
  51.9 2.5 %shard_map.141 = (f32[2048,128]{1,0:T(8,128)}, bf16[240,2048]{1,0:T(8,128)(2,1)}) custom-call(bf16[128,2048]{1,0:T(8,128)(2,1)} %get-tuple-element.6.new, bf16[240,2048]{1,0:T(8,128)(2,1)} %get-tuple-element.7.diag), custom_call_target="tpu_custom_call" | custom-call | tf_op jit(solution)/shard_map/pallas_call | solution.py:833
